TPU v7x, 128 devices: a whole 4x4x4 slice. The times are simulated.
128 devices in a mesh: grp: 4 (over y), ctx: 32 (over x, z, core).
Axes of the slice: x: 4, y: 4, z: 4, core: 2. Of those that a mesh axis runs over, the one named last changes fastest.
Arguments:
- queries: bfloat16 [32768, 1024], P(('grp', 'ctx'))
- key_rows: bfloat16 [32768, 128], P(('grp', 'ctx'))
- value_rows: bfloat16 [32768, 128], P(('grp', 'ctx')), may hold values from -6 to 6
- block_place: int32 [256], P(('grp', 'ctx')), may hold values from 0 to 7, as said below
- document_ids: int32 [4, 8192], P('grp', 'ctx'), may hold values from 0 to 64, as said below
Outputs:
- attended: bfloat16 [32768, 1024], P(('grp', 'ctx'))
Inputs may be any that keep to these rules, and one draw needn't show every extreme that they name: `block_place`: for each index of ctx, the 4 devices with that index hold together each value 0 .. 7 exactly once: every slot of every context group receives exactly one block, and only from devices with the same ctx index. `document_ids`: along each group's positions the labels never fall, so every document is a run of consecutive positions within one group; no document is longer than 4096 tokens, and every group has one of exactly 4096 tokens.
All inputs are finite; a program needn't handle non-finite values.
Results may differ from a plain program's by a relative error of at most 0.0055.
Values may be sent and summed in bfloat16 or wider, within the bound.
A program may use at most 64 MiB of HBM per device.

v0:
```python
import math

import jax
import jax.numpy as jnp
from jax import lax
from jax.sharding import PartitionSpec as P


def select_blocks(picker, rows, block_len):
    count = rows.shape[0] // block_len
    flat = rows.reshape(count, block_len * rows.shape[1])
    chosen = jnp.dot(picker, flat, preferred_element_type=jnp.float32).astype(jnp.bfloat16)
    return chosen.reshape(picker.shape[0] * block_len, rows.shape[1])


def fold_keys(state_in, incoming, query_rows, row_pos, row_doc, scale):
    key_part, value_part, doc_part = incoming
    length = key_part.shape[0]
    head_dim = key_part.shape[1]
    step_len = math.gcd(length, 512)
    steps_count = length // step_len
    key_steps = key_part.reshape(steps_count, step_len, head_dim)
    value_steps = value_part.reshape(steps_count, step_len, head_dim)
    doc_steps = doc_part.reshape(steps_count, step_len)
    step_first = jnp.arange(steps_count, dtype=jnp.int32) * step_len

    def advance(state, inputs):
        row_max, row_sum, weighted = state
        key_block, value_block, doc_block, first_at = inputs
        key_pos = first_at + jnp.arange(step_len, dtype=jnp.int32)
        scores = jnp.dot(query_rows, key_block.T, preferred_element_type=jnp.float32) * scale
        allowed = (
            (key_pos[None, :] <= row_pos[:, None])
            & (key_pos[None, :] >= 0)
            & (doc_block[None, :] == row_doc[:, None])
        )
        scores = jnp.where(allowed, scores, -jnp.inf)
        new_max = jnp.maximum(row_max, jnp.max(scores, axis=1))
        expo = jnp.exp(scores - new_max[:, None])
        rescale = jnp.exp(row_max - new_max)
        new_sum = row_sum * rescale + jnp.sum(expo, axis=1)
        new_weighted = weighted * rescale[:, None] + jnp.dot(
            expo.astype(jnp.bfloat16), value_block, preferred_element_type=jnp.float32
        )
        return ((new_max, new_sum, new_weighted), None)

    result, unused = lax.scan(advance, state_in, (key_steps, value_steps, doc_steps, step_first))
    return result


def on_device(queries, key_rows, value_rows, block_place, document_ids):
    tok_rows = queries.shape[0]
    feat_len = queries.shape[1]
    head_dim = key_rows.shape[1]
    head_count = feat_len // head_dim
    block_count = block_place.shape[0]
    block_len = tok_rows // block_count
    group_count = lax.axis_size("grp")
    my_group = lax.axis_index("grp")
    my_rank = lax.axis_index("ctx")
    slot_ids = jnp.arange(block_count, dtype=jnp.int32)
    every_slot = jnp.arange(group_count * block_count, dtype=jnp.int32)
    all_queries, all_keys, all_values, all_places = (
        lax.all_gather(queries, "grp", axis=0, tiled=True),
        lax.all_gather(key_rows, "grp", axis=0, tiled=True),
        lax.all_gather(value_rows, "grp", axis=0, tiled=True),
        lax.all_gather(block_place, "grp", axis=0, tiled=True),
    )
    picker = (all_places[None, :] == (my_group * block_count + slot_ids)[:, None]).astype(
        jnp.bfloat16
    )
    query_local = select_blocks(picker, all_queries, block_len)
    key_local = select_blocks(picker, all_keys, block_len)
    value_local = select_blocks(picker, all_values, block_len)
    my_docs = document_ids[0]
    query_rows = query_local.reshape(tok_rows * head_count, head_dim)
    row_pos = jnp.repeat(my_rank * tok_rows + jnp.arange(tok_rows, dtype=jnp.int32), head_count)
    row_doc = jnp.repeat(my_docs, head_count)
    scale = head_dim ** (-0.5)
    row_total = tok_rows * head_count
    initial = (
        jnp.full((row_total,), -1e30, jnp.float32),
        jnp.zeros((row_total,), jnp.float32),
        jnp.zeros((row_total, head_dim), jnp.float32),
    )
    final = fold_keys(
        initial,
        (
            lax.all_gather(key_local, "ctx", axis=0, tiled=True),
            lax.all_gather(value_local, "ctx", axis=0, tiled=True),
            lax.all_gather(my_docs, "ctx", axis=0, tiled=True),
        ),
        query_rows,
        row_pos,
        row_doc,
        scale,
    )
    row_max, row_sum, weighted = final
    group_out = (weighted / row_sum[:, None]).astype(jnp.bfloat16).reshape(tok_rows, feat_len)
    all_out = lax.all_gather(group_out, "grp", axis=0, tiled=True)
    backward_pick = (block_place[:, None] == every_slot[None, :]).astype(jnp.bfloat16)
    return select_blocks(backward_pick, all_out, block_len)


def solution(mesh):
    in_specs = (
        P(("grp", "ctx"), None),
        P(("grp", "ctx"), None),
        P(("grp", "ctx"), None),
        P(("grp", "ctx")),
        P("grp", "ctx"),
    )
    out_specs = P(("grp", "ctx"), None)
    return jax.shard_map(
        on_device, mesh=mesh, in_specs=in_specs, out_specs=out_specs, check_vma=False
    )
```

profile of v0, /device:TPU:5, one launch (start us, length us, event | category | flops | bytes accessed | tf_op | source)
XLA Modules:
  0.0 381.7 jit_solution(14089729083383193882)
XLA Ops:
  10.1 7.0 %all-reduce = s32[8]{0:T(128)S(1)} all-reduce(s32[8]{0:T(128)S(1)} %dynamic-update-slice), channel_id=1, replica_groups=mesh['grp'=4,'ctx'=32] {'grp'}, use_global_device_ids=true, to_apply=%add | all-reduce | flops 8 | bytes 64
  17.1 10.7 %all_gather.26 = bf16[1024,128]{1,0:T(8,128)(2,1)S(1)} all-gather(bf16[256,128]{1,0:T(8,128)(2,1)} %param.8), channel_id=1, replica_groups=mesh['grp'=4,'ctx'=32] {'grp'}, dimensions={0}, use_global_device_ids=true | all-gather | bytes 327680 | tf_op jit(solution)/shard_map/all_gather | solution.py:65
  29.0 12.1 %all_gather.29 = bf16[1024,128]{1,0:T(8,128)(2,1)S(1)} all-gather(bf16[256,128]{1,0:T(8,128)(2,1)} %param.9), channel_id=1, replica_groups=mesh['grp'=4,'ctx'=32] {'grp'}, dimensions={0}, use_global_device_ids=true | all-gather | bytes 327680 | tf_op jit(solution)/shard_map/all_gather | solution.py:66
  42.2 30.3 %all-gather = s32[1,8192]{1,0:T(1,128)S(1)} all-gather(s32[1,256]{1,0:T(1,128)} %param.11), channel_id=2, replica_groups=mesh['grp'=4,'ctx'=32] {'ctx'}, dimensions={1}, use_global_device_ids=true | all-gather | bytes 33792 | tf_op jit(solution)/shard_map/all_gather | solution.py:91
  73.8 2.5 reshape.56
  79.3 12.2 %all-gather.6.cloned.1.call-done = bf16[8192,128]{1,0:T(8,128)(2,1)} async-done(((bf16[256,128]{1,0:T(8,128)(2,1)}), bf16[8192,128]{1,0:T(8,128)(2,1)}) %all-gather.6.cloned.1.call-update) | async-done | bytes 2097168 | tf_op jit(solution)/shard_map/all_gather | solution.py:89
  91.5 45.5 %all-gather.10.cloned.1.call-done = bf16[8192,128]{1,0:T(8,128)(2,1)} async-done(((bf16[256,128]{1,0:T(8,128)(2,1)}), bf16[8192,128]{1,0:T(8,128)(2,1)}) %all-gather.10.cloned.1.call-update) | async-done | bytes 2097168 | tf_op jit(solution)/shard_map/all_gather | solution.py:90
  137.1 201.7 %while.15 = (s32[]{:T(128)}, f32[2048]{0:T(1024)S(1)}, f32[2048]{0:T(1024)S(1)}, f32[2048,128]{1,0:T(8,128)S(1)}, s32[16]{0:T(128)S(1)}, /*index=5*/s32[16,512]{...) while((s32[]{:T(128)}, f32[2048]{0:T(1024)S(1)}, ...), condition=%wide.region_3.4_spmd.clone, body=%wide.region_0.3_spmd.clone.sunk | while | flops 549203456 | bytes 32454844 | solution.py:47
  139.4 4.4 %fusion.42 = (f32[2048]{0:T(1024)S(1)}, f32[2048,512]{0,1:T(8,128)}) fusion(bf16[2048,128]{1,0:T(8,128)(2,1)S(1)} %get-tuple-element.241, bf16[16,512,128]{2,1,0:T(8,128)(2,1)} %get-tuple-element.240, s32[]{:T(128)} %get-tuple-element.221, s32[2048]{0:T(1024)S(1)} %eq.98, s32[512]{0:T(512)S(1)} %bitcast.32, ...), kind=kOutput, calls=%fused_computation.42.clone.1 | convolution fusion | flops 275773440 | bytes 4879360 | tf_op jit(solution)/shard_map/while/body/eval_jaxpr/dot_general | solution.py:31
  143.8 2.9 fusion.43
  147.3 2.4 convolution_add_fusion.2
  152.0 4.4 %fusion.42 = (f32[2048]{0:T(1024)S(1)}, f32[2048,512]{0,1:T(8,128)}) fusion(bf16[2048,128]{1,0:T(8,128)(2,1)S(1)} %get-tuple-element.241, bf16[16,512,128]{2,1,0:T(8,128)(2,1)} %get-tuple-element.240, s32[]{:T(128)} %get-tuple-element.221, s32[2048]{0:T(1024)S(1)} %eq.98, s32[512]{0:T(512)S(1)} %bitcast.32, ...), kind=kOutput, calls=%fused_computation.42.clone.1 | convolution fusion | flops 275773440 | bytes 4879360 | tf_op jit(solution)/shard_map/while/body/eval_jaxpr/dot_general | solution.py:31
  156.4 2.9 fusion.43
  164.6 4.4 %fusion.42 = (f32[2048]{0:T(1024)S(1)}, f32[2048,512]{0,1:T(8,128)}) fusion(bf16[2048,128]{1,0:T(8,128)(2,1)S(1)} %get-tuple-element.241, bf16[16,512,128]{2,1,0:T(8,128)(2,1)} %get-tuple-element.240, s32[]{:T(128)} %get-tuple-element.221, s32[2048]{0:T(1024)S(1)} %eq.98, s32[512]{0:T(512)S(1)} %bitcast.32, ...), kind=kOutput, calls=%fused_computation.42.clone.1 | convolution fusion | flops 275773440 | bytes 4879360 | tf_op jit(solution)/shard_map/while/body/eval_jaxpr/dot_general | solution.py:31
  169.0 2.9 fusion.43
  172.5 2.4 convolution_add_fusion.2
  177.2 4.4 %fusion.42 = (f32[2048]{0:T(1024)S(1)}, f32[2048,512]{0,1:T(8,128)}) fusion(bf16[2048,128]{1,0:T(8,128)(2,1)S(1)} %get-tuple-element.241, bf16[16,512,128]{2,1,0:T(8,128)(2,1)} %get-tuple-element.240, s32[]{:T(128)} %get-tuple-element.221, s32[2048]{0:T(1024)S(1)} %eq.98, s32[512]{0:T(512)S(1)} %bitcast.32, ...), kind=kOutput, calls=%fused_computation.42.clone.1 | convolution fusion | flops 275773440 | bytes 4879360 | tf_op jit(solution)/shard_map/while/body/eval_jaxpr/dot_general | solution.py:31
  181.6 2.9 fusion.43
  189.8 4.4 %fusion.42 = (f32[2048]{0:T(1024)S(1)}, f32[2048,512]{0,1:T(8,128)}) fusion(bf16[2048,128]{1,0:T(8,128)(2,1)S(1)} %get-tuple-element.241, bf16[16,512,128]{2,1,0:T(8,128)(2,1)} %get-tuple-element.240, s32[]{:T(128)} %get-tuple-element.221, s32[2048]{0:T(1024)S(1)} %eq.98, s32[512]{0:T(512)S(1)} %bitcast.32, ...), kind=kOutput, calls=%fused_computation.42.clone.1 | convolution fusion | flops 275773440 | bytes 4879360 | tf_op jit(solution)/shard_map/while/body/eval_jaxpr/dot_general | solution.py:31
  194.2 2.9 fusion.43
  197.7 2.4 convolution_add_fusion.2
  202.4 4.4 %fusion.42 = (f32[2048]{0:T(1024)S(1)}, f32[2048,512]{0,1:T(8,128)}) fusion(bf16[2048,128]{1,0:T(8,128)(2,1)S(1)} %get-tuple-element.241, bf16[16,512,128]{2,1,0:T(8,128)(2,1)} %get-tuple-element.240, s32[]{:T(128)} %get-tuple-element.221, s32[2048]{0:T(1024)S(1)} %eq.98, s32[512]{0:T(512)S(1)} %bitcast.32, ...), kind=kOutput, calls=%fused_computation.42.clone.1 | convolution fusion | flops 275773440 | bytes 4879360 | tf_op jit(solution)/shard_map/while/body/eval_jaxpr/dot_general | solution.py:31
  206.8 2.9 fusion.43
  215.0 4.4 %fusion.42 = (f32[2048]{0:T(1024)S(1)}, f32[2048,512]{0,1:T(8,128)}) fusion(bf16[2048,128]{1,0:T(8,128)(2,1)S(1)} %get-tuple-element.241, bf16[16,512,128]{2,1,0:T(8,128)(2,1)} %get-tuple-element.240, s32[]{:T(128)} %get-tuple-element.221, s32[2048]{0:T(1024)S(1)} %eq.98, s32[512]{0:T(512)S(1)} %bitcast.32, ...), kind=kOutput, calls=%fused_computation.42.clone.1 | convolution fusion | flops 275773440 | bytes 4879360 | tf_op jit(solution)/shard_map/while/body/eval_jaxpr/dot_general | solution.py:31
  219.5 2.9 fusion.43
  222.9 2.4 convolution_add_fusion.2
  227.7 4.4 %fusion.42 = (f32[2048]{0:T(1024)S(1)}, f32[2048,512]{0,1:T(8,128)}) fusion(bf16[2048,128]{1,0:T(8,128)(2,1)S(1)} %get-tuple-element.241, bf16[16,512,128]{2,1,0:T(8,128)(2,1)} %get-tuple-element.240, s32[]{:T(128)} %get-tuple-element.221, s32[2048]{0:T(1024)S(1)} %eq.98, s32[512]{0:T(512)S(1)} %bitcast.32, ...), kind=kOutput, calls=%fused_computation.42.clone.1 | convolution fusion | flops 275773440 | bytes 4879360 | tf_op jit(solution)/shard_map/while/body/eval_jaxpr/dot_general | solution.py:31
  232.1 2.9 fusion.43
  240.3 4.4 %fusion.42 = (f32[2048]{0:T(1024)S(1)}, f32[2048,512]{0,1:T(8,128)}) fusion(bf16[2048,128]{1,0:T(8,128)(2,1)S(1)} %get-tuple-element.241, bf16[16,512,128]{2,1,0:T(8,128)(2,1)} %get-tuple-element.240, s32[]{:T(128)} %get-tuple-element.221, s32[2048]{0:T(1024)S(1)} %eq.98, s32[512]{0:T(512)S(1)} %bitcast.32, ...), kind=kOutput, calls=%fused_computation.42.clone.1 | convolution fusion | flops 275773440 | bytes 4879360 | tf_op jit(solution)/shard_map/while/body/eval_jaxpr/dot_general | solution.py:31
  244.7 2.9 fusion.43
  252.9 4.4 %fusion.42 = (f32[2048]{0:T(1024)S(1)}, f32[2048,512]{0,1:T(8,128)}) fusion(bf16[2048,128]{1,0:T(8,128)(2,1)S(1)} %get-tuple-element.241, bf16[16,512,128]{2,1,0:T(8,128)(2,1)} %get-tuple-element.240, s32[]{:T(128)} %get-tuple-element.221, s32[2048]{0:T(1024)S(1)} %eq.98, s32[512]{0:T(512)S(1)} %bitcast.32, ...), kind=kOutput, calls=%fused_computation.42.clone.1 | convolution fusion | flops 275773440 | bytes 4879360 | tf_op jit(solution)/shard_map/while/body/eval_jaxpr/dot_general | solution.py:31
  257.3 2.9 fusion.43
  265.5 4.4 %fusion.42 = (f32[2048]{0:T(1024)S(1)}, f32[2048,512]{0,1:T(8,128)}) fusion(bf16[2048,128]{1,0:T(8,128)(2,1)S(1)} %get-tuple-element.241, bf16[16,512,128]{2,1,0:T(8,128)(2,1)} %get-tuple-element.240, s32[]{:T(128)} %get-tuple-element.221, s32[2048]{0:T(1024)S(1)} %eq.98, s32[512]{0:T(512)S(1)} %bitcast.32, ...), kind=kOutput, calls=%fused_computation.42.clone.1 | convolution fusion | flops 275773440 | bytes 4879360 | tf_op jit(solution)/shard_map/while/body/eval_jaxpr/dot_general | solution.py:31
  269.9 2.9 fusion.43
  273.3 2.4 convolution_add_fusion.2
  278.1 4.4 %fusion.42 = (f32[2048]{0:T(1024)S(1)}, f32[2048,512]{0,1:T(8,128)}) fusion(bf16[2048,128]{1,0:T(8,128)(2,1)S(1)} %get-tuple-element.241, bf16[16,512,128]{2,1,0:T(8,128)(2,1)} %get-tuple-element.240, s32[]{:T(128)} %get-tuple-element.221, s32[2048]{0:T(1024)S(1)} %eq.98, s32[512]{0:T(512)S(1)} %bitcast.32, ...), kind=kOutput, calls=%fused_computation.42.clone.1 | convolution fusion | flops 275773440 | bytes 4879360 | tf_op jit(solution)/shard_map/while/body/eval_jaxpr/dot_general | solution.py:31
  282.5 2.9 fusion.43
  290.7 4.4 %fusion.42 = (f32[2048]{0:T(1024)S(1)}, f32[2048,512]{0,1:T(8,128)}) fusion(bf16[2048,128]{1,0:T(8,128)(2,1)S(1)} %get-tuple-element.241, bf16[16,512,128]{2,1,0:T(8,128)(2,1)} %get-tuple-element.240, s32[]{:T(128)} %get-tuple-element.221, s32[2048]{0:T(1024)S(1)} %eq.98, s32[512]{0:T(512)S(1)} %bitcast.32, ...), kind=kOutput, calls=%fused_computation.42.clone.1 | convolution fusion | flops 275773440 | bytes 4879360 | tf_op jit(solution)/shard_map/while/body/eval_jaxpr/dot_general | solution.py:31
  295.1 2.9 fusion.43
  298.5 2.4 convolution_add_fusion.2
  303.3 4.4 %fusion.42 = (f32[2048]{0:T(1024)S(1)}, f32[2048,512]{0,1:T(8,128)}) fusion(bf16[2048,128]{1,0:T(8,128)(2,1)S(1)} %get-tuple-element.241, bf16[16,512,128]{2,1,0:T(8,128)(2,1)} %get-tuple-element.240, s32[]{:T(128)} %get-tuple-element.221, s32[2048]{0:T(1024)S(1)} %eq.98, s32[512]{0:T(512)S(1)} %bitcast.32, ...), kind=kOutput, calls=%fused_computation.42.clone.1 | convolution fusion | flops 275773440 | bytes 4879360 | tf_op jit(solution)/shard_map/while/body/eval_jaxpr/dot_general | solution.py:31
  307.7 2.9 fusion.43
  315.9 4.4 %fusion.42 = (f32[2048]{0:T(1024)S(1)}, f32[2048,512]{0,1:T(8,128)}) fusion(bf16[2048,128]{1,0:T(8,128)(2,1)S(1)} %get-tuple-element.241, bf16[16,512,128]{2,1,0:T(8,128)(2,1)} %get-tuple-element.240, s32[]{:T(128)} %get-tuple-element.221, s32[2048]{0:T(1024)S(1)} %eq.98, s32[512]{0:T(512)S(1)} %bitcast.32, ...), kind=kOutput, calls=%fused_computation.42.clone.1 | convolution fusion | flops 275773440 | bytes 4879360 | tf_op jit(solution)/shard_map/while/body/eval_jaxpr/dot_general | solution.py:31
  320.3 2.9 fusion.43
  328.5 4.4 %fusion.42 = (f32[2048]{0:T(1024)S(1)}, f32[2048,512]{0,1:T(8,128)}) fusion(bf16[2048,128]{1,0:T(8,128)(2,1)S(1)} %get-tuple-element.241, bf16[16,512,128]{2,1,0:T(8,128)(2,1)} %get-tuple-element.240, s32[]{:T(128)} %get-tuple-element.221, s32[2048]{0:T(1024)S(1)} %eq.98, s32[512]{0:T(512)S(1)} %bitcast.32, ...), kind=kOutput, calls=%fused_computation.42.clone.1 | convolution fusion | flops 275773440 | bytes 4879360 | tf_op jit(solution)/shard_map/while/body/eval_jaxpr/dot_general | solution.py:31
  332.9 2.9 fusion.43
  340.2 30.4 %all-gather.12.cloned.1.call-done = bf16[1024,1024]{1,0:T(8,128)(2,1)} async-done(((bf16[256,1024]{1,0:T(8,128)(2,1)}), bf16[1024,1024]{1,0:T(8,128)(2,1)}) %all-gather.12.cloned.1.call-update) | async-done | bytes 2097168 | tf_op jit(solution)/shard_map/all_gather | solution.py:100
  370.6 2.5 reshape.61
  (255 shorter events, 81.7 us)
Async XLA Ops:
  6.5 67.3 %all-gather.8.cloned.1.call-start = ((), (), s32[]{:S(2)}) async-start(), calls=%async_computation.1 | async-start | bytes 2621440 | tf_op jit(solution)/shard_map/all_gather | solution.py:64
  7.3 84.3 %all-gather.6.cloned.1.call-start = ((), (), s32[]{:S(2)}) async-start(), calls=%async_computation | async-start | bytes 2162688 | tf_op jit(solution)/shard_map/all_gather | solution.py:89
  28.9 108.2 %all-gather.10.cloned.1.call-start = ((), (), s32[]{:S(2)}) async-start(), calls=%async_computation.2 | async-start | bytes 2162688 | tf_op jit(solution)/shard_map/all_gather | solution.py:90
  42.1 328.4 %all-gather.12.cloned.1.call-start = ((), (), s32[]{:S(2)}) async-start(), calls=%async_computation.3 | async-start | bytes 2621440 | tf_op jit(solution)/shard_map/all_gather | solution.py:100
  73.8 63.3 %copy-start.1 = (s32[1,256]{1,0:T(1,128)S(1)}, s32[1,256]{1,0:T(1,128)}, u32[]{:S(2)}) copy-start(s32[1,256]{1,0:T(1,128)} %param.11) | copy-start | bytes 3076
  143.8 3.4 copy-start
  156.4 3.4 copy-start
  169.0 3.4 copy-start
  181.6 3.4 copy-start
  194.2 3.4 copy-start
  206.8 3.4 copy-start
  219.4 3.4 copy-start
  232.1 3.4 copy-start
  244.7 3.4 copy-start
  257.3 3.4 copy-start
  269.9 3.4 copy-start
  282.5 3.4 copy-start
  295.1 3.4 copy-start
  307.7 3.4 copy-start
  320.3 3.4 copy-start
  332.9 3.4 copy-start
  338.8 34.3 %copy-start.2 = (s32[2]{0:T(128)S(1)}, s32[2]{0:T(128)}, u32[]{:S(2)}) copy-start(s32[2]{0:T(128)} %param.10) | copy-start | bytes 28
Sparse Core Ops, SparseCore 0:
  9.0 36.1 all-gather.7
  47.5 43.9 all-gather.5
  93.8 43.2 all-gather.9
  340.3 30.2 all-gather.11
where the time goes:
time: 384 us; the launch traced here: 382 us
  matrix products  111 us (29%)
  waiting for transfers between devices  88.9 us (23%)
  other arithmetic  69 us (18%)
  blocking collectives  60 us (16%)
  local copies, waits for them, and re-layouts  37 us (10%)
  between operations  13.9 us (4%)
    dot_general x16, matrix products, advance(): jnp.dot(query_rows, key_block.T, preferred_element_type=jnp.float32) * scale  70.4 us
    reduce_sum x16, other arithmetic, advance(): new_sum = row_sum * rescale + jnp.sum(expo, axis=1)  46.9 us
    all_gather x1, waiting for transfers between devices, on_device(): lax.all_gather(value_local, 'ctx', axis=0, tiled=True)  45.5 us
    dot_general x16, matrix products, advance(): jnp.dot(expo.astype(jnp.bfloat16), value_block, preferred_element_type=jn...  38.1 us
    all_gather x1, waiting for transfers between devices, on_device(): all_out = lax.all_gather(group_out, 'grp', axis=0, tiled=True)  30.4 us
    all_gather x1, blocking collectives, on_device(): lax.all_gather(my_docs, 'ctx', axis=0, tiled=True)  30.3 us
    all_gather x1, waiting for transfers between devices, on_device(): lax.all_gather(key_local, 'ctx', axis=0, tiled=True)  12.2 us
    all_gather x1, blocking collectives, on_device(): lax.all_gather(value_rows, 'grp', axis=0, tiled=True)  12.1 us
  transfers between devices with their start and end apart: 4, of which 3 were waited for; matrix products, arithmetic and copies ran while one was open for 3% of the time, Pallas kernels for 0%

commit v1 on v0

v1 whole, which is shorter than its diff:
```python
import functools
import math

import jax
import jax.numpy as jnp
from jax import lax
from jax.experimental import pallas as pl
from jax.experimental.pallas import tpu as pltpu
from jax.sharding import PartitionSpec as P

MESH = pl.DeviceIdType.MESH

DH = 128
BLK = 128
ROWS = 544
AUX = 512
CUT = 272
HALF = {"a": (0, 144, CUT), "b": (CUT, 400, ROWS)}
COLS = 9
BIG = 2.0**126
LOWEST = -3.0e38


def rows_of(part):
    first, _, last = HALF[part]
    return pl.ds(first, last - first)


def kernel(q_ref, k_ref, v_ref, place_ref, docs_ref, out_ref, *scratch):
    bufs = scratch[:COLS]
    qa, kb, vb, acc, top, send_sems, recv_sems = scratch[COLS:]
    y = lax.axis_index("grp")
    rank = lax.axis_index("ctx")
    x, z, core = rank // 8, (rank // 2) % 4, rank % 2
    chip = x * 4 + z

    def device(dx=0, dy=0, dz=0, flip=False):
        to_core = 1 - core if flip else core
        to = (((x + dx + 4) % 4) * 4 + (z + dz + 4) % 4) * 2 + to_core
        return ((y + dy + 4) % 4, to)

    friends = [dict(dx=1), dict(dx=-1), dict(dy=1), dict(dy=-1), dict(dz=1), dict(dz=-1), dict(dz=2), dict(flip=True)]
    barrier = pltpu.get_barrier_semaphore()
    for friend in friends:
        pl.semaphore_signal(barrier, inc=1, device_id=device(**friend), device_id_type=MESH)

    mine = bufs[0]
    mine[core, y, pl.ds(0, 128), :] = k_ref[0:128, :].T
    mine[core, y, pl.ds(128, 128), :] = k_ref[128:256, :].T
    mine[core, y, pl.ds(256, 256), :] = v_ref[...]
    row_at = lax.broadcasted_iota(jnp.int32, (32, 128), 0)
    aux = jnp.where(
        row_at == 0,
        docs_ref[0:1, 0:128],
        jnp.where(
            row_at == 1,
            docs_ref[0:1, 128:256],
            jnp.where(row_at == 2, place_ref[0], jnp.where(row_at == 3, place_ref[1], 0)),
        ),
    )
    mine[core, y, pl.ds(AUX, 32), :] = aux.astype(jnp.float32).astype(jnp.bfloat16)

    index_of = {}

    def sem_at(key):
        return index_of.setdefault(key, len(index_of))

    def active(d):
        return chip >= d

    sent = []

    def copy(key, src_d, dst_d, slot, rows, to):
        at = sem_at(key)
        return pltpu.make_async_remote_copy(
            src_ref=bufs[src_d].at[core, slot, rows, :],
            dst_ref=bufs[dst_d].at[core, slot, rows, :],
            send_sem=send_sems.at[at],
            recv_sem=recv_sems.at[at],
            device_id=to,
            device_id_type=MESH,
        )

    def send(key, src_d, dst_d, slot, rows, to, cond):
        c = copy(key, src_d, dst_d, slot, rows, to)

        @pl.when(cond)
        def _():
            c.start()

        sent.append((c, cond))

    waited = set()

    def receive(key, d, slot, rows, cond):
        if key in waited:
            return
        waited.add(key)
        c = copy(key, d, d, slot, rows, device(dx=1))

        @pl.when(cond)
        def _():
            c.wait_recv()

    def slot_of(k):
        return (y + k + 4) % 4

    def along_y(d, part):
        for step in (1, -1):
            send(("y", d, part, step), d, d, y, rows_of(part), device(dy=step), active(d))

    def half(part, step):
        first, mid, last = HALF[part]
        return pl.ds(first, mid - first) if step == 1 else pl.ds(mid, last - mid)

    def pass_y(d, part):
        for step in (1, -1):
            receive(("y", d, part, step), d, slot_of(-step), rows_of(part), active(d))
            send(("yf", d, part, step), d, d, slot_of(-step), half(part, step), device(dy=step), active(d))

    def last_y(d, part):
        for step in (1, -1):
            receive(("yf", d, part, step), d, slot_of(2), half(part, step), active(d))

    def along_x(d, part, k):
        send(("x", d + 4, part, k), d, d + 4, slot_of(k), rows_of(part), device(dx=1), active(d) & (x <= 2))

    def along_z(d, part, k):
        for delta in (1, 3, 2):
            straight = z + delta <= 3
            to = device(dz=delta)
            for wrap in (False, True):
                dst = d + delta - (4 if wrap else 0)
                if dst < 0 or dst > 7 or dst == 6:
                    continue
                ok = active(d) & (jnp.logical_not(straight) if wrap else straight)
                send(("z", dst, part, k), d, dst, slot_of(k), rows_of(part), to, ok)

    def came_by(d):
        return "x" if d in (4, 8, 6) else "z"

    def forward(d, part, k):
        if d in (0, 4, 2):
            along_x(d, part, k)
        if d in (0, 4, 8):
            along_z(d, part, k)

    def take(d, part, k):
        receive((came_by(d), d, part, k), d, slot_of(k), rows_of(part), active(d))

    def take_a(d):
        take(d, "a", 0)
        along_y(d, "a")
        forward(d, "a", 0)

    def take_b(d):
        for k in (0, 1, -1, 2):
            take(d, "b", k)
            forward(d, "b", k)

    def core_copy(d, slot):
        at = sem_at(("c", d))
        return pltpu.make_async_remote_copy(
            src_ref=bufs[d].at[slot],
            dst_ref=bufs[d].at[slot],
            send_sem=send_sems.at[at],
            recv_sem=recv_sems.at[at],
            device_id=device(flip=True),
            device_id_type=MESH,
        )

    def swap(d):
        c = core_copy(d, core)

        @pl.when(active(d))
        def _():
            c.start()

        sent.append((c, active(d)))

    def swapped(d):
        c = core_copy(d, 1 - core)

        @pl.when(active(d))
        def _():
            c.wait_recv()

    factor = DH**-0.5 * math.log2(math.e)

    def stage(d, j):
        buf = bufs[d]
        group = place_ref[j] // 2
        for c in range(2):
            auxes = [buf[c, i, pl.ds(AUX, 32), :].astype(jnp.float32) for i in range(4)]
            for s in range(2):
                target = (group * 2 + s).astype(jnp.float32)
                keys = jnp.zeros((128, 128), jnp.bfloat16)
                values = jnp.zeros((128, 128), jnp.bfloat16)
                labels = jnp.zeros((1, 128), jnp.float32)
                for i in range(4):
                    labels = jnp.where(group == i, auxes[i][s : s + 1, :], labels)
                    for b in range(2):
                        pick = (auxes[i][2 + b : 3 + b, :] == target).astype(jnp.float32).astype(jnp.bfloat16)
                        keys = keys + buf[c, i, pl.ds(b * 128, 128), :] * pick
                        values = values + buf[c, i, pl.ds(256 + b * 128, 128), :] * pick
                at = (c * 2 + s) * 128
                kb[j, pl.ds(0, 128), pl.ds(at, 128)] = keys
                entry = lax.broadcasted_iota(jnp.int32, (128, 128), 0).astype(jnp.float32)
                kb[j, pl.ds(128, 128), pl.ds(at, 128)] = jnp.where(entry == labels, 0.0, -BIG).astype(jnp.bfloat16)
                vb[j, pl.ds(at, 128), pl.ds(0, 128)] = values

    step_rows = 256

    def attend(d, j):
        stage(d, j)
        slot_now = place_ref[j] % 2

        def body(i, carry):
            at = pl.multiple_of(i * step_rows, step_rows)
            rows = pl.ds(at, step_rows)
            scores = jnp.dot(qa[j, rows, :], kb[j], preferred_element_type=jnp.float32)
            if d == 0:
                q_pos = core * 256 + slot_now * 128 + lax.broadcasted_iota(jnp.int32, (step_rows, 512), 0) % 128
                k_pos = lax.broadcasted_iota(jnp.int32, (step_rows, 512), 1)
                scores = jnp.where(k_pos <= q_pos, scores, -BIG)
            old = top[j, rows, :]
            new = jnp.maximum(old, jnp.max(scores, axis=1, keepdims=True))
            weights = jnp.exp2((scores - new[:, 0:1]) * factor).astype(jnp.bfloat16)
            ratio = jnp.exp2((old - new) * factor)
            got = jnp.dot(weights, vb[j], preferred_element_type=jnp.float32)
            acc[j, rows, 0:128] = acc[j, rows, 0:128] * ratio + got[:, 0:128]
            acc[j, rows, 128:256] = acc[j, rows, 128:256] * ratio + got[:, 128:256]
            top[j, rows, :] = new
            return carry

        lax.fori_loop(0, 1024 // step_rows, body, 0)

    def compute(d):
        @pl.when(active(d))
        def _():
            for j in range(2):
                attend(d, j)

    def ready(d):
        for j in range(2):
            group, s = place_ref[j] // 2, place_ref[j] % 2
            labels = jnp.zeros((1, 128), jnp.float32)
            for i in range(4):
                tile = bufs[0][core, i, pl.ds(AUX, 32), :].astype(jnp.float32)
                for slot in range(2):
                    labels = jnp.where((group == i) & (s == slot), tile[slot : slot + 1, :], labels)
            column = jnp.broadcast_to(labels, (128, 128)).T
            entry = lax.broadcasted_iota(jnp.int32, (128, 128), 1).astype(jnp.float32)
            hot = jnp.where(entry == column, 1.0, 0.0).astype(jnp.bfloat16)
            for h in range(8):
                qa[j, pl.ds(h * 128, 128), pl.ds(128, 128)] = hot

    pl.semaphore_wait(barrier, len(friends))

    along_y(0, "a")
    along_y(0, "b")
    forward(0, "a", 0)
    forward(0, "b", 0)

    for j in range(2):
        for h in range(8):
            qa[j, pl.ds(h * 128, 128), pl.ds(0, 128)] = q_ref[pl.ds(j * 128, 128), pl.ds(h * 128, 128)]
    top[...] = jnp.full(top.shape, LOWEST, jnp.float32)
    acc[...] = jnp.zeros(acc.shape, jnp.float32)
    vb[:, :, pl.ds(128, 128)] = jnp.ones((2, 512, 128), jnp.bfloat16)

    def tail(d):
        last_y(d, "a")
        swap(d)

    pass_y(0, "a")
    pass_y(0, "b")
    forward(0, "b", 1)
    forward(0, "b", -1)
    take_a(4)
    take_a(1)
    take_a(3)
    take_a(2)
    last_y(0, "b")
    forward(0, "b", 2)
    tail(0)
    pass_y(4, "a")
    take_a(8)
    pass_y(1, "a")
    ready(0)
    swapped(0)
    compute(0)
    take_b(4)
    pass_y(3, "a")
    tail(4)
    swapped(4)
    compute(4)
    take_b(1)
    take_a(5)
    pass_y(2, "a")
    tail(1)
    take_a(7)
    take_a(6)
    swapped(1)
    compute(1)
    take_b(3)
    pass_y(8, "a")
    tail(3)
    swapped(3)
    compute(3)
    take_b(2)
    pass_y(5, "a")
    tail(2)
    take_b(8)
    swapped(2)
    compute(2)
    pass_y(7, "a")
    tail(8)
    swapped(8)
    compute(8)
    pass_y(6, "a")
    take_b(5)
    tail(5)
    take_b(7)
    tail(7)
    swapped(5)
    compute(5)
    take_b(6)
    tail(6)
    swapped(7)
    compute(7)
    swapped(6)
    compute(6)

    for j in range(2):
        for h in range(8):
            rows = pl.ds(h * 128, 128)
            result = acc[j, rows, 0:128] / acc[j, rows, 128:256]
            out_ref[pl.ds(j * 128, 128), pl.ds(h * 128, 128)] = result.astype(jnp.bfloat16)

    for c, cond in sent:
        pl.when(cond)(c.wait_send)
    assert len(index_of) <= SEMS, len(index_of)


SEMS = 128


def on_device(queries, key_rows, value_rows, block_place, document_ids):
    vmem = pl.BlockSpec(memory_space=pltpu.VMEM)
    smem = pl.BlockSpec(memory_space=pltpu.SMEM)
    scratch = [pltpu.VMEM((2, 4, ROWS, 128), jnp.bfloat16) for _ in range(COLS)]
    scratch += [
        pltpu.VMEM((2, 1024, 256), jnp.bfloat16),
        pltpu.VMEM((2, 256, 512), jnp.bfloat16),
        pltpu.VMEM((2, 512, 256), jnp.bfloat16),
        pltpu.VMEM((2, 1024, 256), jnp.float32),
        pltpu.VMEM((2, 1024, 128), jnp.float32),
        pltpu.SemaphoreType.DMA((SEMS,)),
        pltpu.SemaphoreType.DMA((SEMS,)),
    ]
    return pl.pallas_call(
        kernel,
        out_shape=jax.ShapeDtypeStruct(queries.shape, jnp.bfloat16),
        in_specs=[vmem, vmem, vmem, smem, vmem],
        out_specs=vmem,
        scratch_shapes=scratch,
        compiler_params=pltpu.CompilerParams(collective_id=0, has_side_effects=True, vmem_limit_bytes=56 * 2**20),
    )(queries, key_rows, value_rows, block_place, document_ids)


def solution(mesh):
    rows = P(("grp", "ctx"), None)
    return jax.shard_map(
        on_device,
        mesh=mesh,
        in_specs=(rows, rows, rows, P(("grp", "ctx")), P("grp", "ctx")),
        out_specs=rows,
        check_vma=False,
    )
```

time: 384 us -> 96.4 us (0.25)
  matrix products: 111 us -> 0 us
  Pallas kernels: 0 us -> 93.3 us
  waiting for transfers between devices: 88.9 us -> 0 us
  other arithmetic: 69 us -> 0 us
  blocking collectives: 60 us -> 0 us
  local copies, waits for them, and re-layouts: 37 us -> 1.87 us
  between operations: 13.9 us -> 0.01 us
    dot_general x36 -> x0, matrix products: 111 us -> none  [the longest x16 70.4 us: advance(): jnp.dot(query_rows, key_block.T, preferred_element_type=jnp.float32) * scale]
    pallas_call x0 -> x1, Pallas kernels: none -> 93.3 us  [on_device(): pl.pallas_call(kernel, out_shape=jax.ShapeDtypeStruct(queries.shape, jnp....]
    all_gather x4 -> x0, waiting for transfers between devices: 88.2 us -> none  [the longest x1 45.5 us: on_device(): lax.all_gather(value_local, 'ctx', axis=0, tiled=True)]
    all_gather x3 -> x0, blocking collectives: 53 us -> none  [the longest x1 30.3 us: on_device(): lax.all_gather(my_docs, 'ctx', axis=0, tiled=True)]
    reduce_sum x16 -> x0, other arithmetic: 46.9 us -> none  [advance(): new_sum = row_sum * rescale + jnp.sum(expo, axis=1)]
    add x34 -> x0, other arithmetic: 10.5 us -> none  [the longest x16 10.3 us: advance(): key_pos = first_at + jnp.arange(step_len, dtype=jnp.int32)]
    ge x16 -> x0, other arithmetic: 10.5 us -> none  [advance(): key_pos[None, :] >= 0]
    dynamic_slice x32 -> x0, local copies, waits for them, and re-layouts: 9.58 us -> none  [fold_keys(): lax.scan(advance, state_in, (key_steps, value_steps, doc_steps, step_first))]
  transfers between devices with their start and end apart: 4 -> 0, of which waited for: 3 -> 0; matrix products, arithmetic and copies ran while one was open for 3% -> 0% of each run, Pallas kernels for 0% -> 0%
where the time goes in v1:
time: 96.4 us; the launch traced here: 95.1 us
  Pallas kernels  93.3 us (97%)
  local copies, waits for them, and re-layouts  1.87 us (2%)
    pallas_call x1, Pallas kernels, on_device(): pl.pallas_call(kernel, out_shape=jax.ShapeDtypeStruct(queries.shape, jnp....  93.3 us

profile of v1, /device:TPU:5, one launch (start us, length us, event | category | flops | bytes accessed | tf_op | source)
XLA Modules:
  0.0 95.1 jit_solution(831325170487895951)
XLA Ops:
  0.0 93.3 %shard_map.55 = bf16[256,1024]{1,0:T(8,128)(2,1)} custom-call(bf16[256,1024]{1,0:T(8,128)(2,1)} %q_ref.1, bf16[256,128]{1,0:T(8,128)(2,1)} %k_ref.1, bf16[256,128]{1,0:T(8,128)(2,1)} %v_ref.1, s32[2]{0:T(128)} %place_ref.1, s32[1,256]{1,0:T(1,128)} %docs_ref.1), custom_call_target="tpu_custom_call" | custom-call | tf_op jit(solution)/shard_map/pallas_call | solution.py:362
  93.3 1.9 %copy.7 = bf16[256,1024]{1,0:T(8,128)(2,1)} copy(bf16[256,1024]{1,0:T(8,128)(2,1)} %shard_map.55) | data formatting | bytes 1048576

commit v2 on v1

--- a/solution.py
+++ b/solution.py
@@ -209,20 +209,23 @@
                 kb[j, pl.ds(128, 128), pl.ds(at, 128)] = jnp.where(entry == labels, 0.0, -BIG).astype(jnp.bfloat16)
                 vb[j, pl.ds(at, 128), pl.ds(0, 128)] = values
 
-    step_rows = 256
+    step_rows = 512
 
     def attend(d, j):
         stage(d, j)
         slot_now = place_ref[j] % 2
 
-        def body(i, carry):
-            at = pl.multiple_of(i * step_rows, step_rows)
-            rows = pl.ds(at, step_rows)
+        def score(i):
+            rows = pl.ds(i * step_rows, step_rows)
             scores = jnp.dot(qa[j, rows, :], kb[j], preferred_element_type=jnp.float32)
             if d == 0:
                 q_pos = core * 256 + slot_now * 128 + lax.broadcasted_iota(jnp.int32, (step_rows, 512), 0) % 128
                 k_pos = lax.broadcasted_iota(jnp.int32, (step_rows, 512), 1)
                 scores = jnp.where(k_pos <= q_pos, scores, -BIG)
+            return scores
+
+        def rest(i, scores):
+            rows = pl.ds(i * step_rows, step_rows)
             old = top[j, rows, :]
             new = jnp.maximum(old, jnp.max(scores, axis=1, keepdims=True))
             weights = jnp.exp2((scores - new[:, 0:1]) * factor).astype(jnp.bfloat16)
@@ -231,9 +234,13 @@
             acc[j, rows, 0:128] = acc[j, rows, 0:128] * ratio + got[:, 0:128]
             acc[j, rows, 128:256] = acc[j, rows, 128:256] * ratio + got[:, 128:256]
             top[j, rows, :] = new
-            return carry
-
-        lax.fori_loop(0, 1024 // step_rows, body, 0)
+
+        n = 1024 // step_rows
+        now = score(0)
+        for i in range(n):
+            later = score(i + 1) if i + 1 < n else None
+            rest(i, now)
+            now = later
 
     def compute(d):
         @pl.when(active(d))

time: 96.4 us -> 66.1 us (0.69)
  Pallas kernels: 93.3 us -> 63.7 us
    pallas_call x1, Pallas kernels: 93.3 us -> 63.7 us  [on_device(): pl.pallas_call(kernel, out_shape=jax.ShapeDtypeStruct(queries.shape, jnp....]
where the time goes in v2:
time: 66.1 us; the launch traced here: 65.6 us
  Pallas kernels  63.7 us (96%)
  local copies, waits for them, and re-layouts  1.87 us (3%)
    pallas_call x1, Pallas kernels, on_device(): pl.pallas_call(kernel, out_shape=jax.ShapeDtypeStruct(queries.shape, jnp....  63.7 us
    unnamed x1, local copies, waits for them, and re-layouts  1.87 us

profile of v2, /device:TPU:5, one launch (start us, length us, event | category | flops | bytes accessed | tf_op | source)
XLA Modules:
  0.0 65.6 jit_solution(8742986034021672288)
XLA Ops:
  0.0 63.7 %shard_map.55 = bf16[256,1024]{1,0:T(8,128)(2,1)} custom-call(bf16[256,1024]{1,0:T(8,128)(2,1)} %q_ref.1, bf16[256,128]{1,0:T(8,128)(2,1)} %k_ref.1, bf16[256,128]{1,0:T(8,128)(2,1)} %v_ref.1, s32[2]{0:T(128)} %place_ref.1, s32[1,256]{1,0:T(1,128)} %docs_ref.1), custom_call_target="tpu_custom_call" | custom-call | tf_op jit(solution)/shard_map/pallas_call | solution.py:369
  63.7 1.9 %copy.7 = bf16[256,1024]{1,0:T(8,128)(2,1)} copy(bf16[256,1024]{1,0:T(8,128)(2,1)} %shard_map.55) | data formatting | bytes 1048576

commit v3 on v2

--- a/solution.py
+++ b/solution.py
@@ -12,13 +12,103 @@
 
 DH = 128
 BLK = 128
-ROWS = 544
+ROWS = 528
 AUX = 512
-CUT = 272
-HALF = {"a": (0, 144, CUT), "b": (CUT, 400, ROWS)}
+CUT = 256
+HALF = {"a": (0, 128, CUT), "b": (CUT, 400, ROWS)}
 COLS = 9
 BIG = 2.0**126
 LOWEST = -3.0e38
+
+
+ORDER = (
+    ("along_y", 0, "b"),
+    ("forward", 0, "a", 0),
+    ("along_y", 0, "a"),
+    ("forward", 0, "b", 0),
+    ("take_a", 4),
+    ("pass_y", 0, "b"),
+    ("pass_y", 0, "a"),
+    ("take_b", 4, 0),
+    ("pair",),
+    ("take_a", 8),
+    ("take_b", 1, 0),
+    ("take_a", 3),
+    ("third",),
+    ("take_b", 4, 1),
+    ("take_a", 1),
+    ("tail", 0, "b"),
+    ("pass_y", 4, "a"),
+    ("take_b", 3, 0),
+    ("take_a", 2),
+    ("take_b", 4, -1),
+    ("take_b", 4, 2),
+    ("take_b", 1, 1),
+    ("tail", 0, "a"),
+    ("pass_y", 8, "a"),
+    ("tail", 4, "b"),
+    ("pass_y", 1, "a"),
+    ("take_a", 7),
+    ("take_b", 8, 1),
+    ("take_b", 1, -1),
+    ("take_b", 8, 0),
+    ("tail", 4, "a"),
+    ("comp", (0,), 0),
+    ("tail", 1, "a"),
+    ("take_a", 5),
+    ("tail", 8, "a"),
+    ("comp", (0,), 1),
+    ("pass_y", 3, "a"),
+    ("take_a", 6),
+    ("take_b", 1, 2),
+    ("take_b", 3, 1),
+    ("tail", 1, "b"),
+    ("comp", (1, 4), 0),
+    ("take_b", 3, 2),
+    ("pass_y", 7, "a"),
+    ("take_b", 3, -1),
+    ("pass_y", 2, "a"),
+    ("take_b", 8, -1),
+    ("take_b", 5, 1),
+    ("take_b", 2, 1),
+    ("pass_y", 5, "a"),
+    ("tail", 3, "a"),
+    ("pass_y", 6, "a"),
+    ("take_b", 8, 2),
+    ("tail", 8, "b"),
+    ("tail", 3, "b"),
+    ("take_b", 5, 0),
+    ("comp", (1, 4), 1),
+    ("take_b", 2, 0),
+    ("comp", (3, 8), 0),
+    ("take_b", 7, 0),
+    ("take_b", 5, 2),
+    ("take_b", 5, -1),
+    ("tail", 5, "b"),
+    ("take_b", 2, -1),
+    ("tail", 5, "a"),
+    ("comp", (3, 8), 1),
+    ("tail", 7, "a"),
+    ("take_b", 2, 2),
+    ("tail", 2, "a"),
+    ("take_b", 7, -1),
+    ("comp", (5,), 0),
+    ("take_b", 6, -1),
+    ("tail", 2, "b"),
+    ("tail", 6, "a"),
+    ("comp", (5,), 1),
+    ("take_b", 6, 0),
+    ("take_b", 6, 1),
+    ("take_b", 7, 2),
+    ("take_b", 6, 2),
+    ("tail", 6, "b"),
+    ("take_b", 7, 1),
+    ("comp", (2,), 0),
+    ("tail", 7, "b"),
+    ("comp", (2,), 1),
+    ("comp", (6, 7), 0),
+    ("comp", (6, 7), 1),
+)
 
 
 def rows_of(part):
@@ -48,7 +138,7 @@
     mine[core, y, pl.ds(0, 128), :] = k_ref[0:128, :].T
     mine[core, y, pl.ds(128, 128), :] = k_ref[128:256, :].T
     mine[core, y, pl.ds(256, 256), :] = v_ref[...]
-    row_at = lax.broadcasted_iota(jnp.int32, (32, 128), 0)
+    row_at = lax.broadcasted_iota(jnp.int32, (16, 128), 0)
     aux = jnp.where(
         row_at == 0,
         docs_ref[0:1, 0:128],
@@ -58,7 +148,7 @@
             jnp.where(row_at == 2, place_ref[0], jnp.where(row_at == 3, place_ref[1], 0)),
         ),
     )
-    mine[core, y, pl.ds(AUX, 32), :] = aux.astype(jnp.float32).astype(jnp.bfloat16)
+    mine[core, y, pl.ds(AUX, 16), :] = aux.astype(jnp.float32).astype(jnp.bfloat16)
 
     index_of = {}
 
@@ -153,24 +243,24 @@
         along_y(d, "a")
         forward(d, "a", 0)
 
-    def take_b(d):
-        for k in (0, 1, -1, 2):
-            take(d, "b", k)
-            forward(d, "b", k)
-
-    def core_copy(d, slot):
-        at = sem_at(("c", d))
+    def take_b(d, k):
+        take(d, "b", k)
+        forward(d, "b", k)
+
+    def core_copy(d, part, slot):
+        at = sem_at(("c", d, part))
+        piece = bufs[d].at[slot, :, rows_of(part), :]
         return pltpu.make_async_remote_copy(
-            src_ref=bufs[d].at[slot],
-            dst_ref=bufs[d].at[slot],
+            src_ref=piece,
+            dst_ref=piece,
             send_sem=send_sems.at[at],
             recv_sem=recv_sems.at[at],
             device_id=device(flip=True),
             device_id_type=MESH,
         )
 
-    def swap(d):
-        c = core_copy(d, core)
+    def swap(d, part):
+        c = core_copy(d, part, core)
 
         @pl.when(active(d))
         def _():
@@ -179,48 +269,58 @@
         sent.append((c, active(d)))
 
     def swapped(d):
-        c = core_copy(d, 1 - core)
-
-        @pl.when(active(d))
-        def _():
-            c.wait_recv()
+        for part in ("a", "b"):
+            c = core_copy(d, part, 1 - core)
+            pl.when(active(d))(c.wait_recv)
 
     factor = DH**-0.5 * math.log2(math.e)
 
-    def stage(d, j):
+    def stage(d, base):
         buf = bufs[d]
-        group = place_ref[j] // 2
+        groups = [place_ref[j] // 2 for j in range(2)]
+        entry = lax.broadcasted_iota(jnp.int32, (128, 128), 0).astype(jnp.float32)
         for c in range(2):
-            auxes = [buf[c, i, pl.ds(AUX, 32), :].astype(jnp.float32) for i in range(4)]
-            for s in range(2):
-                target = (group * 2 + s).astype(jnp.float32)
-                keys = jnp.zeros((128, 128), jnp.bfloat16)
-                values = jnp.zeros((128, 128), jnp.bfloat16)
-                labels = jnp.zeros((1, 128), jnp.float32)
+            auxes = [buf[c, i, pl.ds(AUX, 16), :].astype(jnp.float32) for i in range(4)]
+            wanted = [(j, s) for j in range(2) for s in range(2)]
+            picks = {}
+            for i in range(4):
+                for b in range(2):
+                    place = auxes[i][2 + b : 3 + b, :]
+                    for j, s in wanted:
+                        hit = place == (groups[j] * 2 + s).astype(jnp.float32)
+                        picks[i, b, j, s] = hit.astype(jnp.float32).astype(jnp.bfloat16)
+            for first, ref in ((0, kb), (256, vb)):
+                found = {w: None for w in wanted}
                 for i in range(4):
-                    labels = jnp.where(group == i, auxes[i][s : s + 1, :], labels)
                     for b in range(2):
-                        pick = (auxes[i][2 + b : 3 + b, :] == target).astype(jnp.float32).astype(jnp.bfloat16)
-                        keys = keys + buf[c, i, pl.ds(b * 128, 128), :] * pick
-                        values = values + buf[c, i, pl.ds(256 + b * 128, 128), :] * pick
-                at = (c * 2 + s) * 128
-                kb[j, pl.ds(0, 128), pl.ds(at, 128)] = keys
-                entry = lax.broadcasted_iota(jnp.int32, (128, 128), 0).astype(jnp.float32)
-                kb[j, pl.ds(128, 128), pl.ds(at, 128)] = jnp.where(entry == labels, 0.0, -BIG).astype(jnp.bfloat16)
-                vb[j, pl.ds(at, 128), pl.ds(0, 128)] = values
+                        block = buf[c, i, pl.ds(first + b * 128, 128), :]
+                        for w in wanted:
+                            term = block * picks[(i, b) + w]
+                            found[w] = term if found[w] is None else found[w] + term
+                for j, s in wanted:
+                    at = pl.ds(base + (c * 2 + s) * 128, 128)
+                    if first == 0:
+                        kb[j, pl.ds(0, 128), at] = found[j, s]
+                    else:
+                        vb[j, at, pl.ds(0, 128)] = found[j, s]
+            for j, s in wanted:
+                labels = auxes[0][s : s + 1, :]
+                for i in range(1, 4):
+                    labels = jnp.where(groups[j] == i, auxes[i][s : s + 1, :], labels)
+                at = pl.ds(base + (c * 2 + s) * 128, 128)
+                kb[j, pl.ds(128, 128), at] = jnp.where(entry == labels, 0.0, -BIG).astype(jnp.bfloat16)
 
     step_rows = 512
 
-    def attend(d, j):
-        stage(d, j)
-        slot_now = place_ref[j] % 2
+    def attend(ds, j):
+        n_keys = 512 * len(ds)
 
         def score(i):
             rows = pl.ds(i * step_rows, step_rows)
-            scores = jnp.dot(qa[j, rows, :], kb[j], preferred_element_type=jnp.float32)
-            if d == 0:
-                q_pos = core * 256 + slot_now * 128 + lax.broadcasted_iota(jnp.int32, (step_rows, 512), 0) % 128
-                k_pos = lax.broadcasted_iota(jnp.int32, (step_rows, 512), 1)
+            scores = jnp.dot(qa[j, rows, :], kb[j, :, 0:n_keys], preferred_element_type=jnp.float32)
+            if 0 in ds:
+                q_pos = core * 256 + (place_ref[j] % 2) * 128 + lax.broadcasted_iota(jnp.int32, (step_rows, n_keys), 0) % 128
+                k_pos = lax.broadcasted_iota(jnp.int32, (step_rows, n_keys), 1)
                 scores = jnp.where(k_pos <= q_pos, scores, -BIG)
             return scores
 
@@ -230,7 +330,7 @@
             new = jnp.maximum(old, jnp.max(scores, axis=1, keepdims=True))
             weights = jnp.exp2((scores - new[:, 0:1]) * factor).astype(jnp.bfloat16)
             ratio = jnp.exp2((old - new) * factor)
-            got = jnp.dot(weights, vb[j], preferred_element_type=jnp.float32)
+            got = jnp.dot(weights, vb[j, 0:n_keys, :], preferred_element_type=jnp.float32)
             acc[j, rows, 0:128] = acc[j, rows, 0:128] * ratio + got[:, 0:128]
             acc[j, rows, 128:256] = acc[j, rows, 128:256] * ratio + got[:, 128:256]
             top[j, rows, :] = new
@@ -242,18 +342,25 @@
             rest(i, now)
             now = later
 
-    def compute(d):
-        @pl.when(active(d))
-        def _():
-            for j in range(2):
-                attend(d, j)
-
-    def ready(d):
+    def compute(ds, j):
+        def some(ds):
+            if j == 0:
+                for e, d in enumerate(ds):
+                    stage(d, 512 * e)
+            attend(ds, j)
+
+        if len(ds) == 1:
+            pl.when(active(ds[0]))(lambda: some(ds))
+        else:
+            pl.when(active(ds[1]))(lambda: some(ds))
+            pl.when(active(ds[0]) & jnp.logical_not(active(ds[1])))(lambda: some(ds[:1]))
+
+    def ready():
         for j in range(2):
             group, s = place_ref[j] // 2, place_ref[j] % 2
             labels = jnp.zeros((1, 128), jnp.float32)
             for i in range(4):
-                tile = bufs[0][core, i, pl.ds(AUX, 32), :].astype(jnp.float32)
+                tile = bufs[0][core, i, pl.ds(AUX, 16), :].astype(jnp.float32)
                 for slot in range(2):
                     labels = jnp.where((group == i) & (s == slot), tile[slot : slot + 1, :], labels)
             column = jnp.broadcast_to(labels, (128, 128)).T
@@ -264,80 +371,42 @@
 
     pl.semaphore_wait(barrier, len(friends))
 
-    along_y(0, "a")
-    along_y(0, "b")
-    forward(0, "a", 0)
-    forward(0, "b", 0)
-
-    for j in range(2):
-        for h in range(8):
-            qa[j, pl.ds(h * 128, 128), pl.ds(0, 128)] = q_ref[pl.ds(j * 128, 128), pl.ds(h * 128, 128)]
-    top[...] = jnp.full(top.shape, LOWEST, jnp.float32)
-    acc[...] = jnp.zeros(acc.shape, jnp.float32)
-    vb[:, :, pl.ds(128, 128)] = jnp.ones((2, 512, 128), jnp.bfloat16)
-
-    def tail(d):
-        last_y(d, "a")
-        swap(d)
-
-    pass_y(0, "a")
-    pass_y(0, "b")
-    forward(0, "b", 1)
-    forward(0, "b", -1)
-    take_a(4)
-    take_a(1)
-    take_a(3)
-    take_a(2)
-    last_y(0, "b")
-    forward(0, "b", 2)
-    tail(0)
-    pass_y(4, "a")
-    take_a(8)
-    pass_y(1, "a")
-    ready(0)
-    swapped(0)
-    compute(0)
-    take_b(4)
-    pass_y(3, "a")
-    tail(4)
-    swapped(4)
-    compute(4)
-    take_b(1)
-    take_a(5)
-    pass_y(2, "a")
-    tail(1)
-    take_a(7)
-    take_a(6)
-    swapped(1)
-    compute(1)
-    take_b(3)
-    pass_y(8, "a")
-    tail(3)
-    swapped(3)
-    compute(3)
-    take_b(2)
-    pass_y(5, "a")
-    tail(2)
-    take_b(8)
-    swapped(2)
-    compute(2)
-    pass_y(7, "a")
-    tail(8)
-    swapped(8)
-    compute(8)
-    pass_y(6, "a")
-    take_b(5)
-    tail(5)
-    take_b(7)
-    tail(7)
-    swapped(5)
-    compute(5)
-    take_b(6)
-    tail(6)
-    swapped(7)
-    compute(7)
-    swapped(6)
-    compute(6)
+    def local():
+        for j in range(2):
+            for h in range(8):
+                qa[j, pl.ds(h * 128, 128), pl.ds(0, 128)] = q_ref[pl.ds(j * 128, 128), pl.ds(h * 128, 128)]
+        top[...] = jnp.full(top.shape, LOWEST, jnp.float32)
+        acc[...] = jnp.zeros(acc.shape, jnp.float32)
+        vb[:, :, pl.ds(128, 128)] = jnp.ones((2, 1024, 128), jnp.bfloat16)
+
+    def tail(d, part):
+        if part == "a":
+            last_y(d, "a")
+        swap(d, part)
+
+    def pair():
+        forward(0, "b", 1)
+        forward(0, "b", -1)
+
+    def third():
+        last_y(0, "b")
+        forward(0, "b", 2)
+
+    def comp(ds, j):
+        if j == 0:
+            for d in ds:
+                swapped(d)
+            if 0 in ds:
+                ready()
+        compute(ds, j)
+
+    steps = dict(
+        along_y=along_y, pass_y=pass_y, forward=forward, take_a=take_a, take_b=take_b, tail=tail, pair=pair, third=third, comp=comp
+    )
+    for at, (name, *args) in enumerate(ORDER):
+        if at == 4:
+            local()
+        steps[name](*args)
 
     for j in range(2):
         for h in range(8):
@@ -359,8 +428,8 @@
     scratch = [pltpu.VMEM((2, 4, ROWS, 128), jnp.bfloat16) for _ in range(COLS)]
     scratch += [
         pltpu.VMEM((2, 1024, 256), jnp.bfloat16),
-        pltpu.VMEM((2, 256, 512), jnp.bfloat16),
-        pltpu.VMEM((2, 512, 256), jnp.bfloat16),
+        pltpu.VMEM((2, 256, 1024), jnp.bfloat16),
+        pltpu.VMEM((2, 1024, 256), jnp.bfloat16),
         pltpu.VMEM((2, 1024, 256), jnp.float32),
         pltpu.VMEM((2, 1024, 128), jnp.float32),
         pltpu.SemaphoreType.DMA((SEMS,)),

time: 66.1 us -> 56.1 us (0.85)
  Pallas kernels: 63.7 us -> 53.6 us
    pallas_call x1, Pallas kernels: 63.7 us -> 53.6 us  [on_device(): pl.pallas_call(kernel, out_shape=jax.ShapeDtypeStruct(queries.shape, jnp....]
where the time goes in v3:
time: 56.1 us; the launch traced here: 55.5 us
  Pallas kernels  53.6 us (96%)
  local copies, waits for them, and re-layouts  1.87 us (3%)
    pallas_call x1, Pallas kernels, on_device(): pl.pallas_call(kernel, out_shape=jax.ShapeDtypeStruct(queries.shape, jnp....  53.6 us
    unnamed x1, local copies, waits for them, and re-layouts  1.87 us

profile of v3, /device:TPU:5, one launch (start us, length us, event | category | flops | bytes accessed | tf_op | source)
XLA Modules:
  0.0 55.5 jit_solution(9160270977634586262)
XLA Ops:
  0.0 53.6 %shard_map.55 = bf16[256,1024]{1,0:T(8,128)(2,1)} custom-call(bf16[256,1024]{1,0:T(8,128)(2,1)} %q_ref.1, bf16[256,128]{1,0:T(8,128)(2,1)} %k_ref.1, bf16[256,128]{1,0:T(8,128)(2,1)} %v_ref.1, s32[2]{0:T(128)} %place_ref.1, s32[1,256]{1,0:T(1,128)} %docs_ref.1), custom_call_target="tpu_custom_call" | custom-call | tf_op jit(solution)/shard_map/pallas_call | solution.py:438
  53.6 1.9 %copy.7 = bf16[256,1024]{1,0:T(8,128)(2,1)} copy(bf16[256,1024]{1,0:T(8,128)(2,1)} %shard_map.55) | data formatting | bytes 1048576

commit v4 on v3

--- a/solution.py
+++ b/solution.py
@@ -22,89 +22,89 @@
 
 
 ORDER = (
-    ("along_y", 0, "b"),
     ("forward", 0, "a", 0),
     ("along_y", 0, "a"),
     ("forward", 0, "b", 0),
+    ("along_y", 0, "b"),
     ("take_a", 4),
     ("pass_y", 0, "b"),
+    ("pair",),
+    ("take_b", 4, 0),
+    ("take_a", 8),
+    ("take_a", 1),
     ("pass_y", 0, "a"),
-    ("take_b", 4, 0),
-    ("pair",),
-    ("take_a", 8),
+    ("third",),
     ("take_b", 1, 0),
+    ("pass_y", 4, "a"),
+    ("take_b", 4, -1),
+    ("take_b", 4, 1),
+    ("tail", 0, "b"),
+    ("pass_y", 1, "a"),
+    ("tail", 0, "a"),
     ("take_a", 3),
-    ("third",),
-    ("take_b", 4, 1),
-    ("take_a", 1),
-    ("tail", 0, "b"),
-    ("pass_y", 4, "a"),
+    ("tail", 4, "a"),
     ("take_b", 3, 0),
+    ("take_b", 4, 2),
+    ("tail", 1, "a"),
+    ("tail", 4, "b"),
+    ("comp", (0,), 0),
+    ("take_b", 1, 1),
+    ("take_a", 7),
+    ("take_b", 8, 0),
+    ("pass_y", 8, "a"),
+    ("take_a", 5),
+    ("take_b", 1, -1),
+    ("pass_y", 3, "a"),
     ("take_a", 2),
-    ("take_b", 4, -1),
-    ("take_b", 4, 2),
-    ("take_b", 1, 1),
-    ("tail", 0, "a"),
-    ("pass_y", 8, "a"),
-    ("tail", 4, "b"),
-    ("pass_y", 1, "a"),
-    ("take_a", 7),
+    ("comp", (0,), 1),
+    ("take_b", 1, 2),
+    ("tail", 1, "b"),
     ("take_b", 8, 1),
-    ("take_b", 1, -1),
-    ("take_b", 8, 0),
-    ("tail", 4, "a"),
-    ("comp", (0,), 0),
-    ("tail", 1, "a"),
-    ("take_a", 5),
+    ("take_b", 8, 2),
+    ("take_b", 3, -1),
+    ("comp", (1, 4), 0),
+    ("take_b", 3, 1),
+    ("tail", 3, "a"),
+    ("take_b", 8, -1),
+    ("pass_y", 5, "a"),
     ("tail", 8, "a"),
-    ("comp", (0,), 1),
-    ("pass_y", 3, "a"),
+    ("take_b", 3, 2),
     ("take_a", 6),
-    ("take_b", 1, 2),
-    ("take_b", 3, 1),
-    ("tail", 1, "b"),
-    ("comp", (1, 4), 0),
-    ("take_b", 3, 2),
     ("pass_y", 7, "a"),
-    ("take_b", 3, -1),
+    ("tail", 3, "b"),
+    ("tail", 8, "b"),
     ("pass_y", 2, "a"),
-    ("take_b", 8, -1),
+    ("take_b", 2, -1),
+    ("take_b", 7, 0),
+    ("comp", (1, 4), 1),
+    ("take_b", 7, 1),
+    ("take_b", 2, 0),
+    ("take_b", 2, 1),
+    ("take_b", 5, 2),
     ("take_b", 5, 1),
-    ("take_b", 2, 1),
-    ("pass_y", 5, "a"),
-    ("tail", 3, "a"),
-    ("pass_y", 6, "a"),
-    ("take_b", 8, 2),
-    ("tail", 8, "b"),
-    ("tail", 3, "b"),
     ("take_b", 5, 0),
-    ("comp", (1, 4), 1),
-    ("take_b", 2, 0),
     ("comp", (3, 8), 0),
-    ("take_b", 7, 0),
-    ("take_b", 5, 2),
     ("take_b", 5, -1),
-    ("tail", 5, "b"),
-    ("take_b", 2, -1),
-    ("tail", 5, "a"),
-    ("comp", (3, 8), 1),
-    ("tail", 7, "a"),
+    ("take_b", 6, -1),
+    ("take_b", 7, 2),
     ("take_b", 2, 2),
     ("tail", 2, "a"),
+    ("take_b", 6, 0),
+    ("tail", 5, "a"),
+    ("tail", 5, "b"),
+    ("pass_y", 6, "a"),
+    ("comp", (3, 8), 1),
     ("take_b", 7, -1),
+    ("tail", 7, "b"),
+    ("take_b", 6, 1),
+    ("tail", 2, "b"),
     ("comp", (5,), 0),
-    ("take_b", 6, -1),
-    ("tail", 2, "b"),
+    ("take_b", 6, 2),
     ("tail", 6, "a"),
     ("comp", (5,), 1),
-    ("take_b", 6, 0),
-    ("take_b", 6, 1),
-    ("take_b", 7, 2),
-    ("take_b", 6, 2),
+    ("tail", 7, "a"),
     ("tail", 6, "b"),
-    ("take_b", 7, 1),
     ("comp", (2,), 0),
-    ("tail", 7, "b"),
     ("comp", (2,), 1),
     ("comp", (6, 7), 0),
     ("comp", (6, 7), 1),
@@ -121,13 +121,15 @@
     qa, kb, vb, acc, top, send_sems, recv_sems = scratch[COLS:]
     y = lax.axis_index("grp")
     rank = lax.axis_index("ctx")
-    x, z, core = rank // 8, (rank // 2) % 4, rank % 2
+    x, z, core = lax.div(rank, 8), lax.rem(lax.div(rank, 2), 4), lax.rem(rank, 2)
     chip = x * 4 + z
 
+    xs, ys, zs = ([lax.rem(v + k, 4) for k in range(4)] for v in (x, y, z))
+    here = {(a, c): (xs[a] * 4 + zs[c]) * 2 + core for a, c in ((0, 0), (1, 0), (3, 0), (0, 1), (0, 2), (0, 3))}
+    partner = chip * 2 + 1 - core
+
     def device(dx=0, dy=0, dz=0, flip=False):
-        to_core = 1 - core if flip else core
-        to = (((x + dx + 4) % 4) * 4 + (z + dz + 4) % 4) * 2 + to_core
-        return ((y + dy + 4) % 4, to)
+        return (ys[dy % 4], partner if flip else here[dx % 4, dz % 4])
 
     friends = [dict(dx=1), dict(dx=-1), dict(dy=1), dict(dy=-1), dict(dz=1), dict(dz=-1), dict(dz=2), dict(flip=True)]
     barrier = pltpu.get_barrier_semaphore()
@@ -193,7 +195,7 @@
             c.wait_recv()
 
     def slot_of(k):
-        return (y + k + 4) % 4
+        return ys[k % 4]
 
     def along_y(d, part):
         for step in (1, -1):

time: 56.1 us -> 54.5 us (0.971)
  Pallas kernels: 53.6 us -> 52.4 us
    pallas_call x1, Pallas kernels: 53.6 us -> 52.4 us  [on_device(): pl.pallas_call(kernel, out_shape=jax.ShapeDtypeStruct(queries.shape, jnp....]
where the time goes in v4:
time: 54.5 us; the launch traced here: 54.3 us
  Pallas kernels  52.4 us (96%)
  local copies, waits for them, and re-layouts  1.87 us (3%)
    pallas_call x1, Pallas kernels, on_device(): pl.pallas_call(kernel, out_shape=jax.ShapeDtypeStruct(queries.shape, jnp....  52.4 us
    unnamed x1, local copies, waits for them, and re-layouts  1.87 us

profile of v4, /device:TPU:5, one launch (start us, length us, event | category | flops | bytes accessed | tf_op | source)
XLA Modules:
  0.0 54.3 jit_solution(13591890038470219212)
XLA Ops:
  0.0 52.4 %shard_map.55 = bf16[256,1024]{1,0:T(8,128)(2,1)} custom-call(bf16[256,1024]{1,0:T(8,128)(2,1)} %q_ref.1, bf16[256,128]{1,0:T(8,128)(2,1)} %k_ref.1, bf16[256,128]{1,0:T(8,128)(2,1)} %v_ref.1, s32[2]{0:T(128)} %place_ref.1, s32[1,256]{1,0:T(1,128)} %docs_ref.1), custom_call_target="tpu_custom_call" | custom-call | tf_op jit(solution)/shard_map/pallas_call | solution.py:440
  52.5 1.9 %copy.7 = bf16[256,1024]{1,0:T(8,128)(2,1)} copy(bf16[256,1024]{1,0:T(8,128)(2,1)} %shard_map.55) | data formatting | bytes 1048576

commit v5 on v4

--- a/solution.py
+++ b/solution.py
@@ -18,7 +18,6 @@
 HALF = {"a": (0, 128, CUT), "b": (CUT, 400, ROWS)}
 COLS = 9
 BIG = 2.0**126
-LOWEST = -3.0e38
 
 
 ORDER = (
@@ -328,13 +327,17 @@
 
         def rest(i, scores):
             rows = pl.ds(i * step_rows, step_rows)
-            old = top[j, rows, :]
-            new = jnp.maximum(old, jnp.max(scores, axis=1, keepdims=True))
+            high = jnp.max(scores, axis=1, keepdims=True)
+            first = 0 in ds
+            new = jnp.broadcast_to(high, (step_rows, 128)) if first else jnp.maximum(top[j, rows, :], high)
             weights = jnp.exp2((scores - new[:, 0:1]) * factor).astype(jnp.bfloat16)
-            ratio = jnp.exp2((old - new) * factor)
             got = jnp.dot(weights, vb[j, 0:n_keys, :], preferred_element_type=jnp.float32)
-            acc[j, rows, 0:128] = acc[j, rows, 0:128] * ratio + got[:, 0:128]
-            acc[j, rows, 128:256] = acc[j, rows, 128:256] * ratio + got[:, 128:256]
+            if first:
+                acc[j, rows, :] = got
+            else:
+                ratio = jnp.exp2((top[j, rows, :] - new) * factor)
+                acc[j, rows, 0:128] = acc[j, rows, 0:128] * ratio + got[:, 0:128]
+                acc[j, rows, 128:256] = acc[j, rows, 128:256] * ratio + got[:, 128:256]
             top[j, rows, :] = new
 
         n = 1024 // step_rows
@@ -377,8 +380,6 @@
         for j in range(2):
             for h in range(8):
                 qa[j, pl.ds(h * 128, 128), pl.ds(0, 128)] = q_ref[pl.ds(j * 128, 128), pl.ds(h * 128, 128)]
-        top[...] = jnp.full(top.shape, LOWEST, jnp.float32)
-        acc[...] = jnp.zeros(acc.shape, jnp.float32)
         vb[:, :, pl.ds(128, 128)] = jnp.ones((2, 1024, 128), jnp.bfloat16)
 
     def tail(d, part):

time: 54.5 us -> 54.6 us (level)
  no operation moved by 1% of the time
where the time goes in v5:
time: 54.6 us; the launch traced here: 54.4 us
  Pallas kernels  52.5 us (96%)
  local copies, waits for them, and re-layouts  1.87 us (3%)
    pallas_call x1, Pallas kernels, on_device(): pl.pallas_call(kernel, out_shape=jax.ShapeDtypeStruct(queries.shape, jnp....  52.5 us
    unnamed x1, local copies, waits for them, and re-layouts  1.87 us

profile of v5, /device:TPU:5, one launch (start us, length us, event | category | flops | bytes accessed | tf_op | source)
XLA Modules:
  0.0 54.4 jit_solution(5973027288026914874)
XLA Ops:
  0.0 52.5 %shard_map.55 = bf16[256,1024]{1,0:T(8,128)(2,1)} custom-call(bf16[256,1024]{1,0:T(8,128)(2,1)} %q_ref.1, bf16[256,128]{1,0:T(8,128)(2,1)} %k_ref.1, bf16[256,128]{1,0:T(8,128)(2,1)} %v_ref.1, s32[2]{0:T(128)} %place_ref.1, s32[1,256]{1,0:T(1,128)} %docs_ref.1), custom_call_target="tpu_custom_call" | custom-call | tf_op jit(solution)/shard_map/pallas_call | solution.py:441
  52.5 1.9 %copy.7 = bf16[256,1024]{1,0:T(8,128)(2,1)} copy(bf16[256,1024]{1,0:T(8,128)(2,1)} %shard_map.55) | data formatting | bytes 1048576
